TPU v7x, 32 devices: a whole 2x2x4 slice. The times are simulated.
32 devices in a mesh: stretch: 2 (over x), wide: 8 (over z, y), sect: 2 (over core).
Axes of the slice: x: 2, y: 2, z: 4, core: 2. Of those that a mesh axis runs over, the one named last changes fastest.
Arguments:
- genotypes: int32 [2048, 32768], P(('wide', 'sect'), 'stretch'), parts along dimension 1, may hold values from 0 to 2, as said below
- covariates: float32 [20, 2048], P(None, ('wide', 'sect')), may hold values from -5 to 5, as said below
- phenotypes: float32 [64, 2048], P(None, ('wide', 'sect')), may hold values from -3000 to 3000
- variant_weight: float32 [32768], P('stretch'), parts along dimension 0, may hold values from 0.1 to 10
- gene_start: int32 [128], P('stretch'), parts along dimension 0, may hold values from 0 to 16256, as said below
Outputs:
- burden_z: float32 [128, 64], P('stretch'), parts along dimension 0
- skat_z: float32 [128, 64], P('stretch'), parts along dimension 0
There are 2 independent parts, one for each index of `stretch`. A program takes and returns all parts, laid end to end along the dimension named above; an argument that names none is the same for every part. Nothing has to cross between parts.
Inputs may be any that keep to these rules, and one draw needn't show every extreme that they name: `genotypes`: dosages 0, 1 or 2. `covariates`: row 0 is all ones. gene_start[0] = 0 and starts rise in multiples of 128; each gene spans 1 to 4 blocks of 128 variants, some gene exactly 4.
All inputs are finite; a program needn't handle non-finite values.
Results may differ from a plain program's by a relative error of at most 0.0047.
Values may be sent and summed in bfloat16 or wider, within the bound.
A program may use at most 320 MiB of HBM per device.

v0:
```python
import jax
import jax.numpy as jnp
import numpy as np
from jax import lax
from jax.sharding import PartitionSpec as P

BLK = 128
NBLK = 128
MOST_BLOCKS = 4


PRECISE = lax.Precision.HIGHEST


def slot_blocks(gene_start, owners, per_owner, variant_count):
    gene_count = gene_start.shape[0]
    gene_ends = jnp.concatenate([gene_start[1:], jnp.full((1,), variant_count, jnp.int32)])
    gene_sizes = (gene_ends - gene_start) // BLK
    first_block = gene_start // BLK
    slot_gene = np.arange(owners)[:, None] + owners * np.arange(per_owner)[None, :]
    gene_pick = (slot_gene[:, :, None] == np.arange(gene_count)[None, None, :]).astype(np.int32)
    first_slot = jnp.sum(gene_pick * first_block[None, None, :], axis=-1)
    size_slot = jnp.sum(gene_pick * gene_sizes[None, None, :], axis=-1)
    block_offset = jnp.arange(MOST_BLOCKS, dtype=jnp.int32)
    inside = block_offset[None, None, :] < size_slot[:, :, None]
    return jnp.where(inside, first_slot[:, :, None] + block_offset[None, None, :], NBLK)


def pack(matrix_in, slot_table, owners):
    leading = matrix_in.shape[0]
    block_rows = matrix_in.reshape(leading, NBLK, BLK)
    block_rows = jnp.concatenate(
        [block_rows, jnp.zeros((leading, 1, BLK), matrix_in.dtype)], axis=1
    )
    gathered_blocks = jnp.take(block_rows, slot_table.reshape(-1), axis=1)
    return gathered_blocks.reshape(leading, owners, -1)


def owner_weights(variant_weight, slot_table, own_index, per_owner):
    my_slots = lax.dynamic_index_in_dim(slot_table, own_index, 0, keepdims=False)
    weight_blocks = jnp.concatenate(
        [variant_weight.reshape(NBLK, BLK), jnp.zeros((1, BLK), jnp.float32)], axis=0
    )
    return jnp.take(weight_blocks, my_slots.reshape(-1), axis=0).reshape(
        per_owner, MOST_BLOCKS * BLK
    )


def trait_fold(flat_received, shard_piece):
    return jnp.dot(shard_piece, flat_received, preferred_element_type=jnp.float32)


def gene_moments(gene_grams, my_weight):
    burden_var = jnp.einsum("jc,jcd,jd->j", my_weight, gene_grams, my_weight, precision=PRECISE)
    weight_sq = my_weight * my_weight
    null_mean = jnp.sum(weight_sq * jnp.diagonal(gene_grams, axis1=1, axis2=2), axis=1)
    null_var = 2.0 * jnp.einsum(
        "jc,jcd,jd->j", weight_sq, gene_grams * gene_grams, weight_sq, precision=PRECISE
    )
    return (burden_var, null_mean, null_var)


def finish(my_scores, my_weight, gene_grams, sigma_sq, own_index, owners, gene_count):
    per_owner = my_weight.shape[0]
    burden_var, null_mean, null_var = gene_moments(gene_grams, my_weight)
    burden_sum = jnp.einsum("tjc,jc->jt", my_scores, my_weight, precision=PRECISE)
    skat_sum = jnp.einsum(
        "tjc,jc->jt", my_scores * my_scores, my_weight * my_weight, precision=PRECISE
    )
    burden_loc = burden_sum / jnp.sqrt(burden_var[:, None] * sigma_sq[None, :] + 1e-06)
    skat_loc = (skat_sum / sigma_sq[None, :] - null_mean[:, None]) / jnp.sqrt(
        null_var[:, None] + 1e-06
    )
    gene_ids = own_index + owners * jnp.arange(per_owner, dtype=jnp.int32)
    placing = (gene_ids[:, None] == jnp.arange(gene_count, dtype=jnp.int32)[None, :]).astype(
        jnp.float32
    )
    burden_all = jnp.sum(placing[:, :, None] * burden_loc[:, None, :], axis=0)
    skat_all = jnp.sum(placing[:, :, None] * skat_loc[:, None, :], axis=0)
    return (burden_all, skat_all)


def body(genotypes, covariates, phenotypes, variant_weight, gene_start):
    row_count = genotypes.shape[0]
    variant_count = genotypes.shape[1]
    cov_count = covariates.shape[0]
    traits = phenotypes.shape[0]
    gene_count = gene_start.shape[0]
    owners = lax.axis_size("wide")
    sections = lax.axis_size("sect")
    gene_span = MOST_BLOCKS * BLK
    dosage = genotypes.astype(jnp.float32)
    cov_gram = jnp.dot(covariates, covariates.T, precision=PRECISE)
    cov_geno = jnp.dot(covariates, dosage, precision=PRECISE)
    cov_pheno = jnp.dot(covariates, phenotypes.T, precision=PRECISE)
    cov_gram, cov_geno, cov_pheno = lax.psum((cov_gram, cov_geno, cov_pheno), ("wide", "sect"))
    factor = jnp.linalg.cholesky(cov_gram)
    coef_geno = jax.scipy.linalg.cho_solve((factor, True), cov_geno)
    coef_pheno = jax.scipy.linalg.cho_solve((factor, True), cov_pheno)
    resid_geno = (dosage - jnp.dot(covariates.T, coef_geno, precision=PRECISE)).astype(jnp.bfloat16)
    resid_pheno = phenotypes - jnp.dot(coef_pheno.T, covariates, precision=PRECISE)
    residual_sq = lax.psum(jnp.sum(resid_pheno * resid_pheno, axis=1), ("wide", "sect"))
    sigma_sq = residual_sq / (row_count * owners * sections - cov_count)
    pheno_low = resid_pheno.astype(jnp.bfloat16)
    per_owner = -(-gene_count // owners)
    slot_table = slot_blocks(gene_start, owners, per_owner, variant_count)
    send_buffer = pack(resid_geno, slot_table, owners)
    received = lax.all_to_all(send_buffer, "wide", split_axis=1, concat_axis=0, tiled=True)
    flat_received = received.reshape(-1, per_owner * gene_span)
    own_index = lax.axis_index("wide")
    my_weight = owner_weights(variant_weight, slot_table, own_index, per_owner)
    my_scores = trait_fold(flat_received, lax.all_gather(pheno_low, "wide", axis=1, tiled=True))
    my_scores = my_scores.reshape(traits, per_owner, gene_span)
    gene_rows = flat_received.reshape(-1, per_owner, gene_span)
    gene_grams = jnp.einsum(
        "rjc,rjd->jcd", gene_rows, gene_rows, preferred_element_type=jnp.float32
    )
    gene_grams, my_scores = lax.psum((gene_grams, my_scores), "sect")
    burden_all, skat_all = finish(
        my_scores, my_weight, gene_grams, sigma_sq, own_index, owners, gene_count
    )
    burden_z, skat_z = lax.psum((burden_all, skat_all), "wide")
    return (burden_z, skat_z)


def solution(mesh):
    placed = (
        P(("wide", "sect"), "stretch"),
        P(None, ("wide", "sect")),
        P(None, ("wide", "sect")),
        P("stretch"),
        P("stretch"),
    )
    return jax.shard_map(
        body,
        mesh=mesh,
        in_specs=placed,
        out_specs=(P("stretch", None), P("stretch", None)),
        check_vma=False,
    )
```

profile of v0, /device:TPU:0, one launch (start us, length us, event | category | flops | bytes accessed | tf_op | source)
XLA Modules:
  0.0 601.7 jit_solution(2611283113899177471)
XLA Ops:
  7.2 9.0 %copy.52 = s32[128,16384]{0,1:T(8,128)} copy(s32[128,16384]{1,0:T(8,128)} %param.6) | data formatting | bytes 16777216 | tf_op args[0]
  16.3 9.9 %fusion.6 = f32[20,16384]{1,0:T(8,128)} fusion(f32[20,128]{1,0:T(8,128)S(1)} %copy-done, s32[128,16384]{0,1:T(8,128)} %copy.52), kind=kOutput, calls=%fused_computation.10 | convolution fusion | flops 505413632 | bytes 9709568 | tf_op jit(solution)/shard_map/dot_general | solution.py:94
  27.4 63.8 %all-reduce.2 = (f32[20,20]{0,1:T(8,128)S(1)}, f32[20,64]{1,0:T(8,128)S(1)}) all-reduce(f32[20,20]{0,1:T(8,128)S(1)} %fusion.27, f32[20,64]{1,0:T(8,128)S(1)} %fusion.28), channel_id=1, replica_groups=mesh['stretch'=2,'wide'=8,'sect'=2] {'wide','sect'}, use_global_device_ids=true, to_apply=%region_0.0 | all-reduce | flops 1680 | bytes 13440 | tf_op jit(solution)/shard_map/psum | solution.py:96
  91.3 1.8 cholesky.16
  96.1 28.4 %all-reduce.8.cloned.1.call-done = f32[20,16384]{1,0:T(8,128)} async-done(((f32[20,16384]{1,0:T(8,128)}), f32[20,16384]{1,0:T(8,128)}) %all-reduce.8.cloned.1.call-update) | async-done | bytes 1310736 | tf_op jit(solution)/shard_map/psum | solution.py:96
  124.5 2.8 fusion.18
  128.8 15.5 %fusion.1 = bf16[128,16384]{0,1:T(8,128)(2,1)S(1)} fusion(f32[20,16384]{1,0:T(8,128)S(1)} %fusion.16, f32[20,128]{1,0:T(8,128)S(1)} %copy-done, s32[128,16384]{0,1:T(8,128)} %copy.52), kind=kOutput, calls=%fused_computation.5 | convolution fusion | flops 509607936 | bytes 13903872 | tf_op jit(solution)/shard_map/dot_general | solution.py:100
  144.3 2.8 concatenate.14
  147.1 10.7 %gather_fusion = bf16[256,128,128]{1,2,0:T(8,128)(2,1)} fusion(bf16[128,129,128]{0,2,1:T(8,128)(2,1)} %concatenate.14, s32[1024]{0:T(1024)S(1)} %pad_clamp_fusion.1), kind=kCustom, calls=%fused_computation | custom fusion | bytes 16778240 | tf_op jit(solution)/shard_map/jit(_take)/gather | solution.py:35
  157.8 7.7 %broadcast_select_fusion = bf16[128,8,4096]{0,2,1:T(8,128)(2,1)} fusion(bf16[128,8,4096]{0,2,1:T(8,128)(2,1)} %bitcast.99, pred[8,4096]{1,0:T(8,128)(4,1)S(1)} %broadcast_bitcast_fusion), kind=kLoop, calls=%fused_computation.12 | loop fusion | flops 4194304 | bytes 16809984 | tf_op jit(solution)/shard_map/jit(_take)/select_n | solution.py:35
  165.5 5.0 all-to-all-start
  171.3 200.4 %all_gather.3 = bf16[64,1024]{1,0:T(8,128)(2,1)S(1)} all-gather(bf16[64,128]{1,0:T(8,128)(2,1)S(1)} %get-tuple-element.17), channel_id=1, replica_groups=mesh['stretch'=2,'wide'=8,'sect'=2] {'wide'}, dimensions={1}, use_global_device_ids=true | all-gather | bytes 147456 | tf_op jit(solution)/shard_map/all_gather | solution.py:112
  371.7 11.7 %copy.53 = bf16[8,128,1,4096]{3,1,0,2:T(8,128)(2,1)} copy(bf16[8,128,1,4096]{1,3,0,2:T(8,128)(2,1)} %bitcast.12) | data formatting | bytes 16777216 | tf_op jit(solution)/shard_map/all_to_all | solution.py:108
  383.4 12.1 %copy.54 = bf16[4096,1024]{1,0:T(8,128)(2,1)} copy(bf16[4096,1024]{0,1:T(8,128)(2,1)} %bitcast.94) | data formatting | bytes 16777216 | tf_op jit(solution)/shard_map/dot_general | solution.py:50
  395.6 12.2 %copy.74 = bf16[128,8,8,512]{3,2,1,0:T(8,128)(2,1)} copy(bf16[128,8,8,512]{3,1,2,0:T(8,128)(2,1)} %bitcast.95) | data formatting | bytes 16777216
  407.8 21.6 %fusion.2 = f32[8,512,512]{2,1,0:T(8,128)} fusion(bf16[1024,8,512]{2,1,0:T(8,128)(2,1)} %bitcast.100), kind=kOutput, calls=%fused_computation.6 | convolution fusion | flops 4294967296 | bytes 16777216 | tf_op jit(solution)/shard_map/rjc,rjd->jcd/dot_general | solution.py:115
  429.4 7.1 %fusion.11 = f32[64,8,512]{2,0,1:T(8,128)} fusion(bf16[8,512,1024]{2,1,0:T(8,128)(2,1)} %bitcast.98, bf16[64,1024]{1,0:T(8,128)(2,1)S(1)} %all_gather.3), kind=kOutput, calls=%fused_computation.21 | convolution fusion | flops 536870912 | bytes 9568256 | tf_op jit(solution)/shard_map/dot_general | solution.py:50
  437.4 29.7 %psum.61 = f32[64]{0:T(128)S(1)} all-reduce(f32[64]{0:T(128)S(1)} %get-tuple-element.16), channel_id=1, replica_groups=mesh['stretch'=2,'wide'=8,'sect'=2] {'wide','sect'}, use_global_device_ids=true, to_apply=%region_10.11 | all-reduce | flops 64 | bytes 512 | tf_op jit(solution)/shard_map/psum | solution.py:102
  467.2 7.6 %all-reduce.10.cloned.1.call-done = (f32[64,8,512]{2,0,1:T(8,128)}, f32[8,512,512]{2,1,0:T(8,128)}) async-done(((f32[64,8,512]{2,0,1:T(8,128)}, f32[8,512,512]{2,1,0:T(8,128)}), (f32[64,8,512]{2,0,1:T(8,128)}, f32[8,512,512]{2,1,0:T(8,128)})) %all-reduce.10.cloned.1.call-update) | async-done | bytes 9437200 | tf_op jit(solution)/shard_map/psum | solution.py:118
  474.8 59.8 %copy.60 = f32[8,512,512]{0,2,1:T(8,128)} copy(f32[8,512,512]{2,1,0:T(8,128)} %get-tuple-element.11) | data formatting | bytes 16777216 | tf_op jit(solution)/shard_map/psum | solution.py:118
  534.6 5.5 gather_fusion.2
  540.5 6.4 %fusion.30 = f32[8,1,512]{2,1,0:T(1,128)S(1)} fusion(f32[8,512,1]{1,2,0:T(1,128)S(1)} %copy.62, f32[8,512,512]{2,1,0:T(8,128)} %get-tuple-element.11), kind=kOutput, calls=%fused_computation.80 | convolution fusion | flops 25165824 | bytes 8421376 | tf_op jit(solution)/shard_map/jc,jcd,jd->j/dot_general | solution.py:54
  548.0 6.6 %fusion.4 = f32[8,1,512]{2,1,0:T(1,128)S(1)} fusion(f32[8,512,1]{1,2,0:T(1,128)S(1)} %copy.68, f32[8,512,512]{2,1,0:T(8,128)} %get-tuple-element.11), kind=kOutput, calls=%fused_computation.8 | convolution fusion | flops 27262976 | bytes 8421376 | tf_op jit(solution)/shard_map/jc,jcd,jd->j/dot_general | solution.py:57
  556.3 38.4 %all-reduce.3 = (f32[64,64]{1,0:T(8,128)}, f32[64,64]{1,0:T(8,128)}) all-reduce(f32[64,64]{1,0:T(8,128)S(1)} %get-tuple-element.5, f32[64,64]{1,0:T(8,128)S(1)} %get-tuple-element.4), channel_id=1, replica_groups=mesh['stretch'=2,'wide'=8,'sect'=2] {'wide'}, use_global_device_ids=true, to_apply=%region_12.13 | all-reduce | flops 8192 | bytes 65536 | tf_op jit(solution)/shard_map/psum | solution.py:122
  (68 shorter events, 10.5 us)
Async XLA Ops:
  7.2 9.1 %copy-start = (f32[20,128]{1,0:T(8,128)S(1)}, f32[20,128]{1,0:T(8,128)}, u32[]{:S(2)}) copy-start(f32[20,128]{1,0:T(8,128)} %param.7) | copy-start | bytes 30724
  7.2 117.3 %all-reduce.8.cloned.1.call-start = ((), (), s32[]{:S(2)}) async-start(), calls=%async_computation.1 | async-start | bytes 3145728 | tf_op jit(solution)/shard_map/psum | solution.py:96
  16.2 10.1 %copy-start.6 = (s32[64]{0:T(128)S(1)}, s32[64]{0:T(128)}, u32[]{:S(2)}) copy-start(s32[64]{0:T(128)} %param.10) | copy-start | bytes 772
  16.2 10.3 %copy-start.5 = (s32[8,8,64]{2,1,0:T(8,128)S(1)}, s32[8,8,64]{2,1,0:T(8,128)}, u32[]{:S(2)}) copy-start(s32[8,8,64]{2,1,0:T(8,128)} %constant.145.clone) | copy-start | bytes 49156
  16.2 11.0 %copy-start.3 = (f32[64,128]{1,0:T(8,128)S(1)}, f32[64,128]{1,0:T(8,128)}, u32[]{:S(2)}) copy-start(f32[64,128]{1,0:T(8,128)} %param.8) | copy-start | bytes 98308
  165.5 206.2 %all-to-all-start = ((bf16[128,8,4096]{0,2,1:T(8,128)(2,1)}), bf16[128,8,4096]{0,2,1:T(8,128)(2,1)}, u32[]{:S(2)}, u32[]{:S(2)}) async-start(bf16[128,8,4096]{0,2,1:T(8,128)(2,1)} %broadcast_select_fusion), calls=%async_computation | async-start | bytes 16777216 | tf_op jit(solution)/shard_map/all_to_all | solution.py:108
  170.5 304.3 %all-reduce.10.cloned.1.call-start = ((), (), s32[]{:S(2)}) async-start(), calls=%async_computation.2 | async-start | bytes 18874368 | tf_op jit(solution)/shard_map/psum | solution.py:118
  429.4 7.3 %copy-start.4 = (f32[16384]{0:T(1024)S(1)}, f32[16384]{0:T(1024)}, u32[]{:S(2)}) copy-start(f32[16384]{0:T(1024)} %param.9) | copy-start | bytes 196612
  534.6 12.3 %copy-start.2 = (f32[64,8,512]{2,0,1:T(8,128)S(1)}, f32[64,8,512]{2,0,1:T(8,128)}, u32[]{:S(2)}) copy-start(f32[64,8,512]{2,0,1:T(8,128)} %get-tuple-element.10) | copy-start | bytes 3145732
  540.4 54.2 %copy-start.1 = (f32[20,128]{1,0:T(8,128)S(1)}, f32[20,128]{1,0:T(8,128)}, u32[]{:S(2)}) copy-start(f32[20,128]{1,0:T(8,128)} %param.7) | copy-start | bytes 30724
Sparse Core Ops, SparseCore 0:
  26.3 98.1 all-reduce.7
  436.6 38.1 all-reduce.9
where the time goes:
time: 607 us; the launch traced here: 602 us
  blocking collectives  332 us (55%)
  local copies, waits for them, and re-layouts  126 us (21%)
  matrix products  74.4 us (12%)
  waiting for transfers between devices  36 us (6%)
  between operations  14.5 us (2%)
  other arithmetic  13.7 us (2%)
    all_gather x1, blocking collectives, body(): lax.all_gather(pheno_low, 'wide', axis=1, tiled=True)  200 us
    psum x1, blocking collectives, body(): lax.psum((cov_gram, cov_geno, cov_pheno), ('wide', 'sect'))  63.8 us
    psum x1, local copies, waits for them, and re-layouts, body(): gene_grams, my_scores = lax.psum((gene_grams, my_scores), 'sect')  59.8 us
    psum x1, blocking collectives, body(): burden_z, skat_z = lax.psum((burden_all, skat_all), 'wide')  38.4 us
    psum x1, blocking collectives, body(): lax.psum(jnp.sum(resid_pheno * resid_pheno, axis=1), ('wide', 'sect'))  29.7 us
    psum x1, waiting for transfers between devices, body(): lax.psum((cov_gram, cov_geno, cov_pheno), ('wide', 'sect'))  28.4 us
    dot_general x1, matrix products, body(): jnp.einsum('rjc,rjd->jcd', gene_rows, gene_rows, preferred_element_type=j...  21.6 us
    unnamed x18, local copies, waits for them, and re-layouts  21.4 us
  transfers between devices with their start and end apart: 3, of which 2 were waited for; matrix products, arithmetic and copies ran while one was open for 1% of the time, Pallas kernels for 0%

commit v1 on v0

v1 whole, which is shorter than its diff:
```python
import functools

import jax
import jax.numpy as jnp
from jax import lax
from jax.experimental import pallas as pl
from jax.experimental.pallas import tpu as pltpu
from jax.sharding import PartitionSpec as P

BLK = 128
MOST = 4
HALO = MOST - 1
PAD_COV = 24
STAT = 256
F32 = jnp.float32
BF16 = jnp.bfloat16
EXACT = lax.Precision.HIGHEST


def dot(a, b, ca, cb, precision=None):
    return lax.dot_general(
        a, b, (((ca,), (cb,)), ((), ())), precision=precision, preferred_element_type=F32
    )


def kernel(
    n, cov, traits, genes, nb,
    geno, cov_ref, phe_ref, w_ref, bounds_ref,
    burden_ref, skat_ref,
    stage, sendbuf, recv, xloc, xall, cx_send, cx_recv, m_send, m_recv,
    lhs, g_send, g_own, g_recv, z_send, z_own, z_recv, stat_loc, stat_all,
    stage_sem, own_sem, d_send, d_recv, x_send, x_recv, e_send, e_recv, s_send, s_recv,
):
    me = lax.axis_index("wide")
    sect = lax.axis_index("sect")
    lin = me * 2 + sect
    rows = geno.shape[0]
    hb = nb // 2
    width = nb * BLK
    span = (nb + HALO) * BLK
    half = hb * BLK
    half_span = (hb + HALO) * BLK
    dof = rows * n * 2 - cov
    peer = {"sect": 1 - sect}

    def chunk_copy(c):
        cols = pl.ds(pl.multiple_of(c * width, BLK), width)
        return pltpu.make_async_copy(geno.at[:, cols], stage.at[:, cols], stage_sem.at[c])

    def start_chunk(t, carry):
        chunk_copy(lax.rem(me - t + n, n)).start()
        return carry

    lax.fori_loop(0, n, start_chunk, 0)

    xloc[...] = jnp.zeros_like(xloc)
    xloc[0:cov, :] = cov_ref[...]
    xloc[PAD_COV:PAD_COV + traits, :] = phe_ref[...]
    xall[...] = jnp.zeros_like(xall)
    sendbuf[:, n * width:] = jnp.zeros((rows, HALO * BLK), BF16)

    barrier = pltpu.get_barrier_semaphore()

    def greet(q, carry):
        p = lax.rem(lin + q, 2 * n)
        pl.semaphore_signal(
            barrier, inc=1, device_id={"wide": p // 2, "sect": lax.rem(p, 2)},
            device_id_type=pl.DeviceIdType.MESH,
        )
        return carry

    lax.fori_loop(1, 2 * n, greet, 0)
    pl.semaphore_wait(barrier, 2 * n - 1)

    xrows = PAD_COV + traits

    def x_copy(t):
        return pltpu.make_async_remote_copy(
            src_ref=xloc,
            dst_ref=xall.at[0:xrows, pl.ds(pl.multiple_of(me * rows, BLK), rows)],
            send_sem=x_send.at[t], recv_sem=x_recv.at[t],
            device_id={"wide": lax.rem(me - t + n, n)},
            device_id_type=pl.DeviceIdType.MESH,
        )

    def d_copy(t):
        c = lax.rem(me - t + n, n)
        return pltpu.make_async_remote_copy(
            src_ref=sendbuf.at[:, pl.ds(pl.multiple_of(c * width, BLK), span)],
            dst_ref=recv.at[me],
            send_sem=d_send.at[t], recv_sem=d_recv.at[t],
            device_id={"wide": c},
            device_id_type=pl.DeviceIdType.MESH,
        )

    def start_x(t, carry):
        x_copy(t).start()
        return carry

    lax.fori_loop(1, n, start_x, 0)
    xall[0:xrows, pl.ds(pl.multiple_of(me * rows, BLK), rows)] = xloc[...]

    def convert(c):
        chunk_copy(c).wait()
        cols = pl.ds(pl.multiple_of(c * width, BLK), width)
        sendbuf[:, cols] = stage[:, cols].astype(F32).astype(BF16)

    convert(me)

    def send_chunk(t, carry):
        convert(lax.rem(me - t + n, n))
        d_copy(t).start()
        return carry

    lax.fori_loop(1, n, send_chunk, 0)
    own_copy = pltpu.make_async_copy(
        sendbuf.at[:, pl.ds(pl.multiple_of(me * width, BLK), span)], recv.at[me], own_sem
    )
    own_copy.start()

    def wait_x(t, carry):
        x_copy(t).wait()
        return carry

    lax.fori_loop(1, n, wait_x, 0)

    def peer_copy(src, dst, k):
        return pltpu.make_async_remote_copy(
            src_ref=src, dst_ref=dst, send_sem=e_send.at[k], recv_sem=e_recv.at[k],
            device_id=peer, device_id_type=pl.DeviceIdType.MESH,
        )

    call = xall[0:PAD_COV, :]
    cx_send[...] = dot(call, xall[...], 1, 1, EXACT)
    cx_copy = peer_copy(cx_send, cx_recv, 0)
    cx_copy.start()
    cx_copy.wait()
    row = lax.broadcasted_iota(jnp.int32, (PAD_COV, BLK), 0)
    lane = lax.broadcasted_iota(jnp.int32, (PAD_COV, BLK), 1)
    mat = cx_send[...] + cx_recv[...] + jnp.where(lane == row + 96, 1.0, 0.0).astype(F32)
    for j in range(cov):
        scale = 1.0 / jnp.sqrt(mat[j:j + 1, j:j + 1])
        row_j = mat[j:j + 1, :] * scale
        col_j = mat[:, j:j + 1] * scale
        mat = jnp.where(row > j, mat - col_j * row_j, jnp.where(row == j, row_j, mat))
    proj = mat[:, PAD_COV:PAD_COV + traits]
    low_inv = mat[:, 96:96 + PAD_COV]
    cov_unit = dot(low_inv, call, 1, 0, EXACT)
    resid = xall[PAD_COV:PAD_COV + traits, :] - dot(proj, cov_unit, 0, 0, EXACT)
    resid_low = resid.astype(BF16)
    lhs[...] = jnp.zeros_like(lhs)
    lhs[0:traits, :] = resid_low
    hi = cov_unit.astype(BF16)
    rest = cov_unit - hi.astype(F32)
    mid = rest.astype(BF16)
    low = (rest - mid.astype(F32)).astype(BF16)
    lhs[traits:traits + PAD_COV, :] = hi
    lhs[traits + 32:traits + 32 + PAD_COV, :] = mid
    lhs[traits + 64:traits + 64 + PAD_COV, :] = low
    m_send[0:PAD_COV, :] = dot(cov_unit, resid_low.astype(F32), 1, 1, EXACT)
    ones = jnp.ones((8, resid.shape[1]), F32)
    m_send[PAD_COV:PAD_COV + 8, :] = dot(ones, resid * resid, 1, 1, EXACT)
    m_copy = peer_copy(m_send, m_recv, 1)
    m_copy.start()
    m_copy.wait()
    cross = m_send[0:PAD_COV, :] + m_recv[0:PAD_COV, :]
    sigma_sq = (m_send[PAD_COV:PAD_COV + 1, :] + m_recv[PAD_COV:PAD_COV + 1, :]) / dof

    own_copy.wait()

    def wait_d(t, carry):
        d_copy(t).wait()
        return carry

    lax.fori_loop(1, n, wait_d, 0)

    def partial(which, gram, z_out):
        base = which * half

        def one_block(j, carry):
            at = base + j * BLK
            left = recv[:, :, pl.ds(pl.multiple_of(at, BLK), BLK)].reshape(n * rows, BLK)
            right = recv[:, :, pl.ds(pl.multiple_of(at, BLK), MOST * BLK)]
            gram[j] = dot(left, right.reshape(n * rows, MOST * BLK), 0, 0)
            return carry

        lax.fori_loop(0, hb, one_block, 0)

    def partial_z(which, z_out):
        base = pl.multiple_of(which * half, BLK)
        data = recv[:, :, pl.ds(base, half_span)].reshape(n * rows, half_span)
        full = dot(lhs[...], data, 1, 0)
        z_out[0:traits, :] = full[0:traits]
        z_out[traits:traits + 32, :] = (
            full[traits:traits + 32] + full[traits + 32:traits + 64] + full[traits + 64:traits + 96]
        )

    partial(1 - sect, g_send, z_send)
    g_copy = peer_copy(g_send, g_recv, 2)
    g_copy.start()
    partial_z(1 - sect, z_send)
    z_copy = peer_copy(z_send, z_recv, 3)
    z_copy.start()
    partial(sect, g_own, z_own)
    partial_z(sect, z_own)
    z_copy.wait()
    g_copy.wait()

    zs = z_own[...] + z_recv[...]
    z = zs[traits:traits + PAD_COV]
    scores = zs[0:traits, 0:half] - dot(cross, z[:, 0:half], 0, 0, EXACT)

    weight = w_ref[...]
    weight_t = jnp.transpose(
        jnp.concatenate([weight, jnp.zeros((BLK - weight.shape[0], BLK), F32)], axis=0)
    )
    r8 = lax.broadcasted_iota(jnp.int32, (8, BLK), 0)
    l8 = lax.broadcasted_iota(jnp.int32, (8, BLK), 1)
    spread = jnp.concatenate(
        [jnp.where(r8 == j, weight[0:8], 0.0) for j in range(hb)], axis=1
    )
    stat_loc[:, 0:traits] = dot(spread, scores, 1, 1, EXACT)
    stat_loc[:, traits:2 * traits] = dot(spread * spread, scores * scores, 1, 1, EXACT)
    eye = jnp.where(
        lax.broadcasted_iota(jnp.int32, (BLK, BLK), 0)
        == lax.broadcasted_iota(jnp.int32, (BLK, BLK), 1), 1.0, 0.0,
    ).astype(F32)
    lin_rows, sq_rows, diag_rows = [], [], []
    for j in range(hb):
        g = g_own[j] + g_recv[j]
        g = g - dot(z[:, j * BLK:(j + 1) * BLK], z[:, j * BLK:(j + MOST) * BLK], 0, 0, EXACT)
        w_col = weight_t[:, j:j + 1]
        lin_rows.append(jnp.sum(g * w_col, axis=0, keepdims=True))
        sq_rows.append(jnp.sum(g * g * (w_col * w_col), axis=0, keepdims=True))
        diag_rows.append(jnp.sum(g[:, 0:BLK] * eye, axis=0, keepdims=True))
    if hb < 8:
        zero = jnp.zeros((8 - hb, MOST * BLK), F32)
        lin_rows.append(zero)
        sq_rows.append(zero)
        diag_rows.append(zero[:, 0:BLK])
    lin_all = jnp.concatenate(lin_rows, axis=0)
    sq_all = jnp.concatenate(sq_rows, axis=0)
    diag_all = jnp.concatenate(diag_rows, axis=0)
    packed = jnp.zeros((8, BLK), F32)
    for k in range(MOST):
        w_k = weight[k:k + 8]
        twice = 1.0 if k == 0 else 2.0
        first = jnp.sum(lin_all[:, k * BLK:(k + 1) * BLK] * w_k, axis=1, keepdims=True)
        second = jnp.sum(sq_all[:, k * BLK:(k + 1) * BLK] * (w_k * w_k), axis=1, keepdims=True)
        packed = jnp.where(l8 == 2 * k, twice * first, packed)
        packed = jnp.where(l8 == 2 * k + 1, twice * second, packed)
    mean_part = jnp.sum(diag_all * weight[0:8] * weight[0:8], axis=1, keepdims=True)
    packed = jnp.where(l8 == 2 * MOST, mean_part, packed)
    stat_loc[:, 2 * traits:] = packed

    def s_copy(q):
        p = lax.rem(lin + q, 2 * n)
        return pltpu.make_async_remote_copy(
            src_ref=stat_loc,
            dst_ref=stat_all.at[pl.ds(pl.multiple_of(lin * 8, 8), 8)],
            send_sem=s_send.at[q], recv_sem=s_recv.at[q],
            device_id={"wide": p // 2, "sect": lax.rem(p, 2)},
            device_id_type=pl.DeviceIdType.MESH,
        )

    def start_s(q, carry):
        s_copy(q).start()
        return carry

    def wait_s(q, carry):
        s_copy(q).wait()
        return carry

    lax.fori_loop(1, 2 * n, start_s, 0)
    stat_all[pl.ds(pl.multiple_of(lin * 8, 8), 8), :] = stat_loc[...]
    lax.fori_loop(1, 2 * n, wait_s, 0)

    slots = 2 * n * 8
    slot = lax.broadcasted_iota(jnp.int32, (genes, slots), 1)
    within = lax.rem(slot, 8)
    first_variant = ((slot // 8) * hb + within) * BLK
    begin = bounds_ref[:, 0:1]
    end = bounds_ref[:, 1:2]
    member = (within < hb) & (first_variant >= begin) & (first_variant < end)
    sums = dot(jnp.where(member, 1.0, 0.0).astype(F32), stat_all[...], 1, 0, EXACT)
    burden_var = sums[:, 2 * traits:2 * traits + 1]
    null_var = sums[:, 2 * traits + 1:2 * traits + 2]
    null_mean = sums[:, 2 * traits + 2 * MOST:2 * traits + 2 * MOST + 1]
    for k in range(1, MOST):
        inside = member & (first_variant + k * BLK < end)
        pair = dot(
            jnp.where(inside, 1.0, 0.0).astype(F32), stat_all[:, 2 * traits:], 1, 0, EXACT
        )
        burden_var = burden_var + pair[:, 2 * k:2 * k + 1]
        null_var = null_var + pair[:, 2 * k + 1:2 * k + 2]
    null_var = 2.0 * null_var
    burden_ref[...] = sums[:, 0:traits] / jnp.sqrt(burden_var * sigma_sq + 1e-06)
    skat_ref[...] = (sums[:, traits:2 * traits] / sigma_sq - null_mean) / jnp.sqrt(null_var + 1e-06)


def body(genotypes, covariates, phenotypes, variant_weight, gene_start):
    rows, variants = genotypes.shape
    cov = covariates.shape[0]
    traits = phenotypes.shape[0]
    genes = gene_start.shape[0]
    n = lax.axis_size("wide")
    nb = variants // BLK // n
    hb = nb // 2
    span = (nb + HALO) * BLK
    half_span = (hb + HALO) * BLK
    lin = lax.axis_index("wide") * 2 + lax.axis_index("sect")
    padded = jnp.concatenate(
        [variant_weight.reshape(-1, BLK), jnp.zeros((16, BLK), F32)], axis=0
    )
    weight = lax.dynamic_slice(padded, (lin * hb, 0), (16, BLK))
    ends = jnp.concatenate([gene_start[1:], jnp.full((1,), variants, jnp.int32)])
    bounds = jnp.stack([gene_start, ends], axis=1)
    vmem = pl.BlockSpec(memory_space=pltpu.VMEM)
    samples = n * rows
    dma = pltpu.SemaphoreType.DMA
    return pl.pallas_call(
        functools.partial(kernel, n, cov, traits, genes, nb),
        out_shape=(
            jax.ShapeDtypeStruct((genes, traits), F32),
            jax.ShapeDtypeStruct((genes, traits), F32),
        ),
        in_specs=[pl.BlockSpec(memory_space=pl.ANY), vmem, vmem, vmem, vmem],
        out_specs=(vmem, vmem),
        scratch_shapes=[
            pltpu.VMEM((rows, variants), jnp.int32),
            pltpu.VMEM((rows, variants + HALO * BLK), BF16),
            pltpu.VMEM((n, rows, span), BF16),
            pltpu.VMEM((PAD_COV + traits, rows), F32),
            pltpu.VMEM((BLK, samples), F32),
            pltpu.VMEM((PAD_COV, BLK), F32),
            pltpu.VMEM((PAD_COV, BLK), F32),
            pltpu.VMEM((PAD_COV + 8, traits), F32),
            pltpu.VMEM((PAD_COV + 8, traits), F32),
            pltpu.VMEM((traits + 96, samples), BF16),
            pltpu.VMEM((hb, BLK, MOST * BLK), F32),
            pltpu.VMEM((hb, BLK, MOST * BLK), F32),
            pltpu.VMEM((hb, BLK, MOST * BLK), F32),
            pltpu.VMEM((traits + 32, half_span), F32),
            pltpu.VMEM((traits + 32, half_span), F32),
            pltpu.VMEM((traits + 32, half_span), F32),
            pltpu.VMEM((8, STAT), F32),
            pltpu.VMEM((2 * n * 8, STAT), F32),
            dma((n,)), dma, dma((n,)), dma((n,)), dma((n,)), dma((n,)),
            dma((4,)), dma((4,)), dma((2 * n,)), dma((2 * n,)),
        ],
        compiler_params=pltpu.CompilerParams(
            collective_id=0, has_side_effects=True, vmem_limit_bytes=56 * 1024 * 1024
        ),
        cost_estimate=pl.CostEstimate(
            flops=4 * samples * nb * BLK * MOST * BLK,
            bytes_accessed=rows * variants * 4, transcendentals=0,
        ),
    )(genotypes, covariates, phenotypes, weight, bounds)


def solution(mesh):
    placed = (
        P(("wide", "sect"), "stretch"),
        P(None, ("wide", "sect")),
        P(None, ("wide", "sect")),
        P("stretch"),
        P("stretch"),
    )
    return jax.shard_map(
        body,
        mesh=mesh,
        in_specs=placed,
        out_specs=(P("stretch", None), P("stretch", None)),
        check_vma=False,
    )
```

time: 607 us -> 147 us (0.24)
  blocking collectives: 332 us -> 0 us
  Pallas kernels: 0 us -> 140 us
  local copies, waits for them, and re-layouts: 126 us -> 5.48 us
  matrix products: 74.4 us -> 0 us
  waiting for transfers between devices: 36 us -> 0 us
  between operations: 14.5 us -> 0.65 us
  other arithmetic: 13.7 us -> 0.74 us
    all_gather x1 -> x0, blocking collectives: 200 us -> none  [body(): lax.all_gather(pheno_low, 'wide', axis=1, tiled=True)]
    pallas_call x0 -> x1, Pallas kernels: none -> 140 us  [body(): pl.pallas_call(functools.partial(kernel, n, cov, traits, genes, nb), out_...]
    psum x3 -> x0, blocking collectives: 132 us -> none  [the longest x1 63.8 us: body(): lax.psum((cov_gram, cov_geno, cov_pheno), ('wide', 'sect'))]
    dot_general x11 -> x0, matrix products: 69.8 us -> none  [the longest x1 21.6 us: body(): jnp.einsum('rjc,rjd->jcd', gene_rows, gene_rows, preferred_element_type=j...]
    psum x2 -> x0, local copies, waits for them, and re-layouts: 59.9 us -> none  [the longest x1 59.8 us: body(): gene_grams, my_scores = lax.psum((gene_grams, my_scores), 'sect')]
    psum x2 -> x0, waiting for transfers between devices: 36 us -> none  [the longest x1 28.4 us: body(): lax.psum((cov_gram, cov_geno, cov_pheno), ('wide', 'sect'))]
    unnamed x18 -> x2, local copies, waits for them, and re-layouts: 21.4 us -> 2.75 us
    gather x5 -> x0, local copies, waits for them, and re-layouts: 16.9 us -> none  [the longest x1 10.7 us: pack(): gathered_blocks = jnp.take(block_rows, slot_table.reshape(-1), axis=1)]
  transfers between devices with their start and end apart: 3 -> 0, of which waited for: 2 -> 0; matrix products, arithmetic and copies ran while one was open for 1% -> 0% of each run, Pallas kernels for 0% -> 0%
where the time goes in v1:
time: 147 us
  Pallas kernels  140 us (95%)
  local copies, waits for them, and re-layouts  5.48 us (4%)
    pallas_call x1, Pallas kernels, body(): pl.pallas_call(functools.partial(kernel, n, cov, traits, genes, nb), out_...  140 us

profile of v1, /device:TPU:0, one launch (start us, length us, event | category | flops | bytes accessed | tf_op | source)
XLA Modules:
  0.0 146.9 jit_solution(6730630969460434820)
XLA Ops:
  0.6 0.7 slice.3
  1.4 0.1 add_bitcast_fusion
  1.4 0.7 pad_add_fusion
  2.1 1.3 pad_dynamic-slice_fusion.w_ref
  3.4 0.7 copy.9.bounds_ref
  4.1 140.1 %shard_map.68 = (f32[64,64]{1,0:T(8,128)}, f32[64,64]{1,0:T(8,128)}) custom-call(s32[128,16384]{1,0:T(8,128)} %geno.1, f32[20,128]{1,0:T(8,128)} %cov_ref.1, f32[64,128]{1,0:T(8,128)} %phe_ref.1, f32[16,128]{1,0:T(8,128)} %pad_dynamic-slice_fusion.w_ref, s32[64,2]{1,0:T(8,128)} %copy.9.bounds_ref), custom_call_target="tpu_custom_call" | custom-call | flops 4294967296 | bytes 8388608 | tf_op jit(solution)/shard_map/pallas_call | solution.py:321
  144.2 1.4 copy.12
  145.6 1.4 copy.13

commit v2 on v1

--- a/solution.py
+++ b/solution.py
@@ -28,12 +28,18 @@
     geno, cov_ref, phe_ref, w_ref, bounds_ref,
     burden_ref, skat_ref,
     stage, sendbuf, recv, xloc, xall, cx_send, cx_recv, m_send, m_recv,
-    lhs, g_send, g_own, g_recv, z_send, z_own, z_recv, stat_loc, stat_all,
-    stage_sem, own_sem, d_send, d_recv, x_send, x_recv, e_send, e_recv, s_send, s_recv,
+    lhs, g_send, g_own, g_recv, s_send, s_own, sc_recv, z_send, z_own, z_recv, stat_loc, stat_all,
+    stage_sem, own_sem, d_send, d_recv, x_send, x_recv, e_send, e_recv, t_send, t_recv, gs_sem, gr_sem,
 ):
-    me = lax.axis_index("wide")
-    sect = lax.axis_index("sect")
-    lin = me * 2 + sect
+    wide = lax.axis_index("wide")
+    member = n // 2
+    side = wide // member
+    me = lax.rem(wide, member) * 2 + lax.axis_index("sect")
+    lin = me * 2 + side
+
+    def place(group, at_side):
+        return {"wide": at_side * member + group // 2, "sect": lax.rem(group, 2)}
+
     rows = geno.shape[0]
     hb = nb // 2
     width = nb * BLK
@@ -41,7 +47,7 @@
     half = hb * BLK
     half_span = (hb + HALO) * BLK
     dof = rows * n * 2 - cov
-    peer = {"sect": 1 - sect}
+    peer = {"wide": (1 - side) * member + lax.rem(wide, member)}
 
     def chunk_copy(c):
         cols = pl.ds(pl.multiple_of(c * width, BLK), width)
@@ -64,7 +70,7 @@
     def greet(q, carry):
         p = lax.rem(lin + q, 2 * n)
         pl.semaphore_signal(
-            barrier, inc=1, device_id={"wide": p // 2, "sect": lax.rem(p, 2)},
+            barrier, inc=1, device_id=place(p // 2, lax.rem(p, 2)),
             device_id_type=pl.DeviceIdType.MESH,
         )
         return carry
@@ -79,19 +85,25 @@
             src_ref=xloc,
             dst_ref=xall.at[0:xrows, pl.ds(pl.multiple_of(me * rows, BLK), rows)],
             send_sem=x_send.at[t], recv_sem=x_recv.at[t],
-            device_id={"wide": lax.rem(me - t + n, n)},
+            device_id=place(lax.rem(me - t + n, n), side),
             device_id_type=pl.DeviceIdType.MESH,
         )
 
-    def d_copy(t):
+    def d_part(t, part, offset, size):
         c = lax.rem(me - t + n, n)
         return pltpu.make_async_remote_copy(
-            src_ref=sendbuf.at[:, pl.ds(pl.multiple_of(c * width, BLK), span)],
-            dst_ref=recv.at[me],
-            send_sem=d_send.at[t], recv_sem=d_recv.at[t],
-            device_id={"wide": c},
+            src_ref=sendbuf.at[:, pl.ds(pl.multiple_of(c * width + offset, BLK), size)],
+            dst_ref=recv.at[me, :, pl.ds(pl.multiple_of(offset, BLK), size)],
+            send_sem=d_send.at[part, t], recv_sem=d_recv.at[part, t],
+            device_id=place(c, side),
             device_id_type=pl.DeviceIdType.MESH,
         )
+
+    def d_first(t):
+        return d_part(t, 0, (1 - side) * half, half_span)
+
+    def d_second(t):
+        return d_part(t, 1, side * half_span, half)
 
     def start_x(t, carry):
         x_copy(t).start()
@@ -109,10 +121,15 @@
 
     def send_chunk(t, carry):
         convert(lax.rem(me - t + n, n))
-        d_copy(t).start()
+        d_first(t).start()
+        return carry
+
+    def send_second(t, carry):
+        d_second(t).start()
         return carry
 
     lax.fori_loop(1, n, send_chunk, 0)
+    lax.fori_loop(1, n, send_second, 0)
     own_copy = pltpu.make_async_copy(
         sendbuf.at[:, pl.ds(pl.multiple_of(me * width, BLK), span)], recv.at[me], own_sem
     )
@@ -156,6 +173,7 @@
     low = (rest - mid.astype(F32)).astype(BF16)
     lhs[traits:traits + PAD_COV, :] = hi
     lhs[traits + 32:traits + 32 + PAD_COV, :] = mid
+    lhs[traits + 24:traits + 32, :] = jnp.ones((8, lhs.shape[1]), BF16)
     lhs[traits + 64:traits + 64 + PAD_COV, :] = low
     m_send[0:PAD_COV, :] = dot(cov_unit, resid_low.astype(F32), 1, 1, EXACT)
     ones = jnp.ones((8, resid.shape[1]), F32)
@@ -168,47 +186,82 @@
 
     own_copy.wait()
 
-    def wait_d(t, carry):
-        d_copy(t).wait()
-        return carry
-
-    lax.fori_loop(1, n, wait_d, 0)
-
-    def partial(which, gram, z_out):
-        base = which * half
-
-        def one_block(j, carry):
-            at = base + j * BLK
-            left = recv[:, :, pl.ds(pl.multiple_of(at, BLK), BLK)].reshape(n * rows, BLK)
-            right = recv[:, :, pl.ds(pl.multiple_of(at, BLK), MOST * BLK)]
-            gram[j] = dot(left, right.reshape(n * rows, MOST * BLK), 0, 0)
-            return carry
-
-        lax.fori_loop(0, hb, one_block, 0)
-
-    def partial_z(which, z_out):
+    def wait_first(t, carry):
+        d_first(t).wait()
+        return carry
+
+    def wait_second(t, carry):
+        d_second(t).wait()
+        return carry
+
+    def gram(which, j):
+        at = pl.multiple_of(which * half + j * BLK, BLK)
+        left = recv[:, :, pl.ds(at, BLK)].reshape(n * rows, BLK)
+        right = recv[:, :, pl.ds(at, MOST * BLK)].reshape(n * rows, MOST * BLK)
+        return dot(left, right, 0, 0)
+
+    def project(which, s_out, z_out):
         base = pl.multiple_of(which * half, BLK)
         data = recv[:, :, pl.ds(base, half_span)].reshape(n * rows, half_span)
         full = dot(lhs[...], data, 1, 0)
-        z_out[0:traits, :] = full[0:traits]
-        z_out[traits:traits + 32, :] = (
+        s_out[...] = full[0:traits, 0:half]
+        z_out[...] = (
             full[traits:traits + 32] + full[traits + 32:traits + 64] + full[traits + 64:traits + 96]
         )
 
-    partial(1 - sect, g_send, z_send)
-    g_copy = peer_copy(g_send, g_recv, 2)
-    g_copy.start()
-    partial_z(1 - sect, z_send)
-    z_copy = peer_copy(z_send, z_recv, 3)
+    shrink = 1.0 / float(n * rows) ** 0.5
+
+    def g_copy(j):
+        return pltpu.make_async_remote_copy(
+            src_ref=g_send.at[j], dst_ref=g_recv.at[j],
+            send_sem=gs_sem.at[j], recv_sem=gr_sem.at[j],
+            device_id=peer, device_id_type=pl.DeviceIdType.MESH,
+        )
+
+    lax.fori_loop(1, n, wait_first, 0)
+    project(1 - side, s_send, z_send)
+    z_copy = peer_copy(z_send, z_recv, 2)
     z_copy.start()
-    partial(sect, g_own, z_own)
-    partial_z(sect, z_own)
+    sum_row = lax.broadcasted_iota(jnp.int32, (8, half_span), 0) == 0
+
+    def send_gram(j, carry):
+        left = z_send[PAD_COV:32, pl.ds(pl.multiple_of(j * BLK, BLK), BLK)]
+        right = z_send[PAD_COV:32, pl.ds(pl.multiple_of(j * BLK, BLK), MOST * BLK)]
+        left = jnp.where(sum_row[:, 0:BLK], left * shrink, 0.0)
+        right = jnp.where(sum_row[:, 0:MOST * BLK], right * shrink, 0.0)
+        g_send[j] = (gram(1 - side, j) - dot(left, right, 0, 0, EXACT)).astype(BF16)
+        g_copy(j).start()
+        return carry
+
+    lax.fori_loop(0, hb, send_gram, 0)
+    s_part = peer_copy(s_send, sc_recv, 3)
+    s_part.start()
+
+    lax.fori_loop(1, n, wait_second, 0)
+    project(side, s_own, z_own)
+
+    def keep_gram(j, carry):
+        g_own[j] = gram(side, j)
+        return carry
+
+    lax.fori_loop(0, hb, keep_gram, 0)
     z_copy.wait()
-    g_copy.wait()
-
-    zs = z_own[...] + z_recv[...]
-    z = zs[traits:traits + PAD_COV]
-    scores = zs[0:traits, 0:half] - dot(cross, z[:, 0:half], 0, 0, EXACT)
+
+    def wait_gram(j, carry):
+        g_copy(j).wait()
+        return carry
+
+    z = z_own[0:PAD_COV, :] + z_recv[0:PAD_COV, :]
+    shift = jnp.where(sum_row, z_recv[PAD_COV:32, :] * shrink, 0.0)
+    z_minus = jnp.concatenate([-z, shift], axis=0)
+    z_plus = jnp.concatenate([z, shift], axis=0)
+    for j in range(hb):
+        g_own[j] += dot(
+            z_minus[:, j * BLK:(j + 1) * BLK], z_plus[:, j * BLK:(j + MOST) * BLK], 0, 0, EXACT
+        )
+    lax.fori_loop(0, hb, wait_gram, 0)
+    s_part.wait()
+    scores = s_own[...] + sc_recv[...] - dot(cross, z[:, 0:half], 0, 0, EXACT)
 
     weight = w_ref[...]
     weight_t = jnp.transpose(
@@ -227,8 +280,7 @@
     ).astype(F32)
     lin_rows, sq_rows, diag_rows = [], [], []
     for j in range(hb):
-        g = g_own[j] + g_recv[j]
-        g = g - dot(z[:, j * BLK:(j + 1) * BLK], z[:, j * BLK:(j + MOST) * BLK], 0, 0, EXACT)
+        g = g_own[j] + g_recv[j].astype(F32)
         w_col = weight_t[:, j:j + 1]
         lin_rows.append(jnp.sum(g * w_col, axis=0, keepdims=True))
         sq_rows.append(jnp.sum(g * g * (w_col * w_col), axis=0, keepdims=True))
@@ -258,8 +310,8 @@
         return pltpu.make_async_remote_copy(
             src_ref=stat_loc,
             dst_ref=stat_all.at[pl.ds(pl.multiple_of(lin * 8, 8), 8)],
-            send_sem=s_send.at[q], recv_sem=s_recv.at[q],
-            device_id={"wide": p // 2, "sect": lax.rem(p, 2)},
+            send_sem=t_send.at[q], recv_sem=t_recv.at[q],
+            device_id=place(p // 2, lax.rem(p, 2)),
             device_id_type=pl.DeviceIdType.MESH,
         )
 
@@ -281,13 +333,13 @@
     first_variant = ((slot // 8) * hb + within) * BLK
     begin = bounds_ref[:, 0:1]
     end = bounds_ref[:, 1:2]
-    member = (within < hb) & (first_variant >= begin) & (first_variant < end)
-    sums = dot(jnp.where(member, 1.0, 0.0).astype(F32), stat_all[...], 1, 0, EXACT)
+    inside_gene = (within < hb) & (first_variant >= begin) & (first_variant < end)
+    sums = dot(jnp.where(inside_gene, 1.0, 0.0).astype(F32), stat_all[...], 1, 0, EXACT)
     burden_var = sums[:, 2 * traits:2 * traits + 1]
     null_var = sums[:, 2 * traits + 1:2 * traits + 2]
     null_mean = sums[:, 2 * traits + 2 * MOST:2 * traits + 2 * MOST + 1]
     for k in range(1, MOST):
-        inside = member & (first_variant + k * BLK < end)
+        inside = inside_gene & (first_variant + k * BLK < end)
         pair = dot(
             jnp.where(inside, 1.0, 0.0).astype(F32), stat_all[:, 2 * traits:], 1, 0, EXACT
         )
@@ -308,7 +360,8 @@
     hb = nb // 2
     span = (nb + HALO) * BLK
     half_span = (hb + HALO) * BLK
-    lin = lax.axis_index("wide") * 2 + lax.axis_index("sect")
+    wide = lax.axis_index("wide")
+    lin = (lax.rem(wide, n // 2) * 2 + lax.axis_index("sect")) * 2 + wide // (n // 2)
     padded = jnp.concatenate(
         [variant_weight.reshape(-1, BLK), jnp.zeros((16, BLK), F32)], axis=0
     )
@@ -337,16 +390,19 @@
             pltpu.VMEM((PAD_COV + 8, traits), F32),
             pltpu.VMEM((PAD_COV + 8, traits), F32),
             pltpu.VMEM((traits + 96, samples), BF16),
+            pltpu.VMEM((hb, BLK, MOST * BLK), BF16),
             pltpu.VMEM((hb, BLK, MOST * BLK), F32),
-            pltpu.VMEM((hb, BLK, MOST * BLK), F32),
-            pltpu.VMEM((hb, BLK, MOST * BLK), F32),
-            pltpu.VMEM((traits + 32, half_span), F32),
-            pltpu.VMEM((traits + 32, half_span), F32),
-            pltpu.VMEM((traits + 32, half_span), F32),
+            pltpu.VMEM((hb, BLK, MOST * BLK), BF16),
+            pltpu.VMEM((traits, hb * BLK), F32),
+            pltpu.VMEM((traits, hb * BLK), F32),
+            pltpu.VMEM((traits, hb * BLK), F32),
+            pltpu.VMEM((32, half_span), F32),
+            pltpu.VMEM((32, half_span), F32),
+            pltpu.VMEM((32, half_span), F32),
             pltpu.VMEM((8, STAT), F32),
             pltpu.VMEM((2 * n * 8, STAT), F32),
-            dma((n,)), dma, dma((n,)), dma((n,)), dma((n,)), dma((n,)),
-            dma((4,)), dma((4,)), dma((2 * n,)), dma((2 * n,)),
+            dma((n,)), dma, dma((2, n)), dma((2, n)), dma((n,)), dma((n,)),
+            dma((4,)), dma((4,)), dma((2 * n,)), dma((2 * n,)), dma((hb,)), dma((hb,)),
         ],
         compiler_params=pltpu.CompilerParams(
             collective_id=0, has_side_effects=True, vmem_limit_bytes=56 * 1024 * 1024

time: 147 us -> 151 us (1.027)
  Pallas kernels: 140 us -> 144 us
    pallas_call x1, Pallas kernels: 140 us -> 144 us  [body(): pl.pallas_call(functools.partial(kernel, n, cov, traits, genes, nb), out_...]
where the time goes in v2:
time: 151 us
  Pallas kernels  144 us (95%)
  local copies, waits for them, and re-layouts  5.48 us (4%)
    pallas_call x1, Pallas kernels, body(): pl.pallas_call(functools.partial(kernel, n, cov, traits, genes, nb), out_...  144 us

profile of v2, /device:TPU:0, one launch (start us, length us, event | category | flops | bytes accessed | tf_op | source)
XLA Modules:
  0.0 150.9 jit_solution(10449840569253735016)
XLA Ops:
  0.7 0.7 slice.3
  1.4 0.1 add_bitcast_fusion
  1.5 0.7 pad_add_fusion
  2.1 1.3 pad_dynamic-slice_fusion.w_ref
  3.4 0.7 copy.9.bounds_ref
  4.1 144.0 %shard_map.68 = (f32[64,64]{1,0:T(8,128)}, f32[64,64]{1,0:T(8,128)}) custom-call(s32[128,16384]{1,0:T(8,128)} %geno.1, f32[20,128]{1,0:T(8,128)} %cov_ref.1, f32[64,128]{1,0:T(8,128)} %phe_ref.1, f32[16,128]{1,0:T(8,128)} %pad_dynamic-slice_fusion.w_ref, s32[64,2]{1,0:T(8,128)} %copy.9.bounds_ref), custom_call_target="tpu_custom_call" | custom-call | flops 4294967296 | bytes 8388608 | tf_op jit(solution)/shard_map/pallas_call | solution.py:374
  148.1 1.4 copy.12
  149.5 1.4 copy.13

commit v3 on v2

--- a/solution.py
+++ b/solution.py
@@ -23,13 +23,24 @@
     )
 
 
+def slots_of(hb):
+    groups = []
+    for j in range(hb):
+        groups.append([(j, 1)] + ([(j + 1, 3)] if j + 1 < hb else []))
+    for j in range(hb):
+        if j % 4 < 2:
+            groups.append([(j, 2)] + ([(j + 2, 2)] if j + 2 < hb else []))
+    groups.append([(0, 3)])
+    return groups
+
+
 def kernel(
     n, cov, traits, genes, nb,
-    geno, cov_ref, phe_ref, w_ref, bounds_ref,
+    geno, cov_ref, phe_ref, w_ref, start_ref,
     burden_ref, skat_ref,
-    stage, sendbuf, recv, xloc, xall, cx_send, cx_recv, m_send, m_recv,
+    stage, sendbuf, recv, xloc, xall, cx_send, cx_all, w_all, m_send, m_recv,
     lhs, g_send, g_own, g_recv, s_send, s_own, sc_recv, z_send, z_own, z_recv, stat_loc, stat_all,
-    stage_sem, own_sem, d_send, d_recv, x_send, x_recv, e_send, e_recv, t_send, t_recv, gs_sem, gr_sem,
+    stage_sem, own_sem, d_send, d_recv, x_send, x_recv, e_send, e_recv, t_send, t_recv, gs_sem, gr_sem, c_send, c_recv,
 ):
     wide = lax.axis_index("wide")
     member = n // 2
@@ -63,6 +74,9 @@
     xloc[0:cov, :] = cov_ref[...]
     xloc[PAD_COV:PAD_COV + traits, :] = phe_ref[...]
     xall[...] = jnp.zeros_like(xall)
+    blocks = w_ref.shape[0]
+    w_all[0:blocks, :] = w_ref[...]
+    w_all[blocks:, :] = jnp.zeros((16, BLK), F32)
     sendbuf[:, n * width:] = jnp.zeros((rows, HALO * BLK), BF16)
 
     barrier = pltpu.get_barrier_semaphore()
@@ -82,7 +96,7 @@
 
     def x_copy(t):
         return pltpu.make_async_remote_copy(
-            src_ref=xloc,
+            src_ref=xloc.at[0:xrows],
             dst_ref=xall.at[0:xrows, pl.ds(pl.multiple_of(me * rows, BLK), rows)],
             send_sem=x_send.at[t], recv_sem=x_recv.at[t],
             device_id=place(lax.rem(me - t + n, n), side),
@@ -110,7 +124,28 @@
         return carry
 
     lax.fori_loop(1, n, start_x, 0)
-    xall[0:xrows, pl.ds(pl.multiple_of(me * rows, BLK), rows)] = xloc[...]
+    xall[0:xrows, pl.ds(pl.multiple_of(me * rows, BLK), rows)] = xloc[0:xrows, :]
+
+    def c_copy(q):
+        p = lax.rem(lin + q, 2 * n)
+        return pltpu.make_async_remote_copy(
+            src_ref=cx_send, dst_ref=cx_all.at[lin],
+            send_sem=c_send.at[q], recv_sem=c_recv.at[q],
+            device_id=place(p // 2, lax.rem(p, 2)),
+            device_id_type=pl.DeviceIdType.MESH,
+        )
+
+    def start_c(q, carry):
+        c_copy(q).start()
+        return carry
+
+    def wait_c(q, carry):
+        c_copy(q).wait()
+        return carry
+
+    cx_send[...] = dot(xloc[0:PAD_COV, :], xloc[...], 1, 1, EXACT)
+    lax.fori_loop(1, 2 * n, start_c, 0)
+    cx_all[lin] = cx_send[...]
 
     def convert(c):
         chunk_copy(c).wait()
@@ -129,7 +164,6 @@
         return carry
 
     lax.fori_loop(1, n, send_chunk, 0)
-    lax.fori_loop(1, n, send_second, 0)
     own_copy = pltpu.make_async_copy(
         sendbuf.at[:, pl.ds(pl.multiple_of(me * width, BLK), span)], recv.at[me], own_sem
     )
@@ -148,13 +182,10 @@
         )
 
     call = xall[0:PAD_COV, :]
-    cx_send[...] = dot(call, xall[...], 1, 1, EXACT)
-    cx_copy = peer_copy(cx_send, cx_recv, 0)
-    cx_copy.start()
-    cx_copy.wait()
+    lax.fori_loop(1, 2 * n, wait_c, 0)
     row = lax.broadcasted_iota(jnp.int32, (PAD_COV, BLK), 0)
     lane = lax.broadcasted_iota(jnp.int32, (PAD_COV, BLK), 1)
-    mat = cx_send[...] + cx_recv[...] + jnp.where(lane == row + 96, 1.0, 0.0).astype(F32)
+    mat = jnp.sum(cx_all[...], axis=0) + jnp.where(lane == row + 96, 1.0, 0.0).astype(F32)
     for j in range(cov):
         scale = 1.0 / jnp.sqrt(mat[j:j + 1, j:j + 1])
         row_j = mat[j:j + 1, :] * scale
@@ -178,12 +209,8 @@
     m_send[0:PAD_COV, :] = dot(cov_unit, resid_low.astype(F32), 1, 1, EXACT)
     ones = jnp.ones((8, resid.shape[1]), F32)
     m_send[PAD_COV:PAD_COV + 8, :] = dot(ones, resid * resid, 1, 1, EXACT)
-    m_copy = peer_copy(m_send, m_recv, 1)
+    m_copy = peer_copy(m_send, m_recv, 0)
     m_copy.start()
-    m_copy.wait()
-    cross = m_send[0:PAD_COV, :] + m_recv[0:PAD_COV, :]
-    sigma_sq = (m_send[PAD_COV:PAD_COV + 1, :] + m_recv[PAD_COV:PAD_COV + 1, :]) / dof
-
     own_copy.wait()
 
     def wait_first(t, carry):
@@ -211,7 +238,7 @@
 
     shrink = 1.0 / float(n * rows) ** 0.5
 
-    def g_copy(j):
+    def diag_copy(j):
         return pltpu.make_async_remote_copy(
             src_ref=g_send.at[j], dst_ref=g_recv.at[j],
             send_sem=gs_sem.at[j], recv_sem=gr_sem.at[j],
@@ -220,7 +247,7 @@
 
     lax.fori_loop(1, n, wait_first, 0)
     project(1 - side, s_send, z_send)
-    z_copy = peer_copy(z_send, z_recv, 2)
+    z_copy = peer_copy(z_send, z_recv, 1)
     z_copy.start()
     sum_row = lax.broadcasted_iota(jnp.int32, (8, half_span), 0) == 0
 
@@ -229,13 +256,39 @@
         right = z_send[PAD_COV:32, pl.ds(pl.multiple_of(j * BLK, BLK), MOST * BLK)]
         left = jnp.where(sum_row[:, 0:BLK], left * shrink, 0.0)
         right = jnp.where(sum_row[:, 0:MOST * BLK], right * shrink, 0.0)
-        g_send[j] = (gram(1 - side, j) - dot(left, right, 0, 0, EXACT)).astype(BF16)
-        g_copy(j).start()
+        centred = gram(1 - side, j) - dot(left, right, 0, 0, EXACT)
+        g_send[j] = centred[:, 0:BLK].astype(BF16)
+        diag_copy(j).start()
+        g_own[j] = centred
         return carry
 
     lax.fori_loop(0, hb, send_gram, 0)
-    s_part = peer_copy(s_send, sc_recv, 3)
+    start_row = jnp.broadcast_to(start_ref[...], (genes, genes)).astype(F32)
+    gene_r = lax.broadcasted_iota(jnp.int32, (genes, genes), 0)
+    gene_c = lax.broadcasted_iota(jnp.int32, (genes, genes), 1)
+    begin = jnp.sum(jnp.where(gene_c == gene_r, start_row, 0.0), axis=1, keepdims=True)
+    end = jnp.sum(jnp.where(gene_c == gene_r + 1, start_row, 0.0), axis=1, keepdims=True)
+    end = jnp.where(gene_r[:, 0:1] == genes - 1, float(n * width), end)
+    begin = begin.astype(jnp.int32)
+    end = end.astype(jnp.int32)
+    peer_first = (
+        me * nb + (1 - side) * hb + lax.broadcasted_iota(jnp.int32, (genes, BLK), 1)
+    ) * BLK
+    same = [None]
+    for k in range(1, MOST):
+        both = (peer_first >= begin) & (peer_first + k * BLK < end)
+        same.append(jnp.sum(jnp.where(both, 1.0, 0.0).astype(F32), axis=0, keepdims=True))
+    for index, pairs in enumerate(slots_of(hb)):
+        total = None
+        for j, k in pairs:
+            term = g_own[j, :, k * BLK:(k + 1) * BLK] * same[k][:, j:j + 1]
+            total = term if total is None else total + term
+        g_send[hb + index] = total.astype(BF16)
+    g_rest = peer_copy(g_send.at[hb:], g_recv.at[hb:], 3)
+    g_rest.start()
+    s_part = peer_copy(s_send, sc_recv, 2)
     s_part.start()
+    lax.fori_loop(1, n, send_second, 0)
 
     lax.fori_loop(1, n, wait_second, 0)
     project(side, s_own, z_own)
@@ -248,7 +301,7 @@
     z_copy.wait()
 
     def wait_gram(j, carry):
-        g_copy(j).wait()
+        diag_copy(j).wait()
         return carry
 
     z = z_own[0:PAD_COV, :] + z_recv[0:PAD_COV, :]
@@ -260,10 +313,15 @@
             z_minus[:, j * BLK:(j + 1) * BLK], z_plus[:, j * BLK:(j + MOST) * BLK], 0, 0, EXACT
         )
     lax.fori_loop(0, hb, wait_gram, 0)
+    g_rest.wait()
+    where_is = {pair: hb + i for i, pairs in enumerate(slots_of(hb)) for pair in pairs}
     s_part.wait()
+    m_copy.wait()
+    cross = m_send[0:PAD_COV, :] + m_recv[0:PAD_COV, :]
+    sigma_sq = (m_send[PAD_COV:PAD_COV + 1, :] + m_recv[PAD_COV:PAD_COV + 1, :]) / dof
     scores = s_own[...] + sc_recv[...] - dot(cross, z[:, 0:half], 0, 0, EXACT)
 
-    weight = w_ref[...]
+    weight = w_all[pl.ds(lin * hb, 16), :]
     weight_t = jnp.transpose(
         jnp.concatenate([weight, jnp.zeros((BLK - weight.shape[0], BLK), F32)], axis=0)
     )
@@ -280,7 +338,9 @@
     ).astype(F32)
     lin_rows, sq_rows, diag_rows = [], [], []
     for j in range(hb):
-        g = g_own[j] + g_recv[j].astype(F32)
+        g = g_own[j] + jnp.concatenate(
+            [g_recv[j]] + [g_recv[where_is[j, k]] for k in range(1, MOST)], axis=1
+        ).astype(F32)
         w_col = weight_t[:, j:j + 1]
         lin_rows.append(jnp.sum(g * w_col, axis=0, keepdims=True))
         sq_rows.append(jnp.sum(g * g * (w_col * w_col), axis=0, keepdims=True))
@@ -331,8 +391,6 @@
     slot = lax.broadcasted_iota(jnp.int32, (genes, slots), 1)
     within = lax.rem(slot, 8)
     first_variant = ((slot // 8) * hb + within) * BLK
-    begin = bounds_ref[:, 0:1]
-    end = bounds_ref[:, 1:2]
     inside_gene = (within < hb) & (first_variant >= begin) & (first_variant < end)
     sums = dot(jnp.where(inside_gene, 1.0, 0.0).astype(F32), stat_all[...], 1, 0, EXACT)
     burden_var = sums[:, 2 * traits:2 * traits + 1]
@@ -360,14 +418,6 @@
     hb = nb // 2
     span = (nb + HALO) * BLK
     half_span = (hb + HALO) * BLK
-    wide = lax.axis_index("wide")
-    lin = (lax.rem(wide, n // 2) * 2 + lax.axis_index("sect")) * 2 + wide // (n // 2)
-    padded = jnp.concatenate(
-        [variant_weight.reshape(-1, BLK), jnp.zeros((16, BLK), F32)], axis=0
-    )
-    weight = lax.dynamic_slice(padded, (lin * hb, 0), (16, BLK))
-    ends = jnp.concatenate([gene_start[1:], jnp.full((1,), variants, jnp.int32)])
-    bounds = jnp.stack([gene_start, ends], axis=1)
     vmem = pl.BlockSpec(memory_space=pltpu.VMEM)
     samples = n * rows
     dma = pltpu.SemaphoreType.DMA
@@ -383,16 +433,17 @@
             pltpu.VMEM((rows, variants), jnp.int32),
             pltpu.VMEM((rows, variants + HALO * BLK), BF16),
             pltpu.VMEM((n, rows, span), BF16),
-            pltpu.VMEM((PAD_COV + traits, rows), F32),
+            pltpu.VMEM((BLK, rows), F32),
             pltpu.VMEM((BLK, samples), F32),
             pltpu.VMEM((PAD_COV, BLK), F32),
-            pltpu.VMEM((PAD_COV, BLK), F32),
+            pltpu.VMEM((2 * n, PAD_COV, BLK), F32),
+            pltpu.VMEM((variants // BLK + 16, BLK), F32),
             pltpu.VMEM((PAD_COV + 8, traits), F32),
             pltpu.VMEM((PAD_COV + 8, traits), F32),
             pltpu.VMEM((traits + 96, samples), BF16),
-            pltpu.VMEM((hb, BLK, MOST * BLK), BF16),
+            pltpu.VMEM((hb + len(slots_of(hb)), BLK, BLK), BF16),
             pltpu.VMEM((hb, BLK, MOST * BLK), F32),
-            pltpu.VMEM((hb, BLK, MOST * BLK), BF16),
+            pltpu.VMEM((hb + len(slots_of(hb)), BLK, BLK), BF16),
             pltpu.VMEM((traits, hb * BLK), F32),
             pltpu.VMEM((traits, hb * BLK), F32),
             pltpu.VMEM((traits, hb * BLK), F32),
@@ -403,6 +454,7 @@
             pltpu.VMEM((2 * n * 8, STAT), F32),
             dma((n,)), dma, dma((2, n)), dma((2, n)), dma((n,)), dma((n,)),
             dma((4,)), dma((4,)), dma((2 * n,)), dma((2 * n,)), dma((hb,)), dma((hb,)),
+            dma((2 * n,)), dma((2 * n,)),
         ],
         compiler_params=pltpu.CompilerParams(
             collective_id=0, has_side_effects=True, vmem_limit_bytes=56 * 1024 * 1024
@@ -411,7 +463,7 @@
             flops=4 * samples * nb * BLK * MOST * BLK,
             bytes_accessed=rows * variants * 4, transcendentals=0,
         ),
-    )(genotypes, covariates, phenotypes, weight, bounds)
+    )(genotypes, covariates, phenotypes, variant_weight.reshape(-1, BLK), gene_start.reshape(1, genes))
 
 
 def solution(mesh):

time: 151 us -> 115 us (0.76)
  Pallas kernels: 144 us -> 112 us
  local copies, waits for them, and re-layouts: 5.48 us -> 2.75 us
    pallas_call x1, Pallas kernels: 144 us -> 112 us  [body(): pl.pallas_call(functools.partial(kernel, n, cov, traits, genes, nb), out_...]
where the time goes in v3:
time: 115 us
  Pallas kernels  112 us (97%)
  local copies, waits for them, and re-layouts  2.75 us (2%)
    pallas_call x1, Pallas kernels, body(): pl.pallas_call(functools.partial(kernel, n, cov, traits, genes, nb), out_...  112 us
    unnamed x2, local copies, waits for them, and re-layouts  2.75 us

profile of v3, /device:TPU:0, one launch (start us, length us, event | category | flops | bytes accessed | tf_op | source)
XLA Modules:
  0.0 115.1 jit_solution(3235407069789189506)
XLA Ops:
  0.6 111.8 %shard_map.68 = (f32[64,64]{1,0:T(8,128)}, f32[64,64]{1,0:T(8,128)}) custom-call(s32[128,16384]{1,0:T(8,128)} %geno.1, f32[20,128]{1,0:T(8,128)} %cov_ref.1, f32[64,128]{1,0:T(8,128)} %phe_ref.1, f32[128,128]{1,0:T(8,128)} %bitcast.2, s32[1,64]{1,0:T(1,128)} %bitcast.3), custom_call_target="tpu_custom_call" | custom-call | flops 4294967296 | bytes 8388608 | tf_op jit(solution)/shard_map/pallas_call | solution.py:424
  112.4 1.4 %copy.9 = f32[64,64]{1,0:T(8,128)} copy(f32[64,64]{1,0:T(8,128)} %get-tuple-element.4) | data formatting | bytes 32768
  113.8 1.4 %copy.10 = f32[64,64]{1,0:T(8,128)} copy(f32[64,64]{1,0:T(8,128)} %get-tuple-element.5) | data formatting | bytes 32768
